TPU v7x, 128 devices: a whole 4x4x4 slice. The times are simulated.
128 devices in a mesh: seq: 16 (over z, y), head: 2 (over core), clip: 4 (over x).
Axes of the slice: x: 4, y: 4, z: 4, core: 2. Of those that a mesh axis runs over, the one named last changes fastest.
Arguments:
- queries: bfloat16 [4, 2048, 2560], P('clip', 'seq', 'head'), may hold values from -5000 to 5000
- keys: bfloat16 [4, 2048, 2560], P('clip', 'seq', 'head'), may hold values from -5000 to 5000
- values: bfloat16 [4, 2048, 2560], P('clip', 'seq', 'head'), may hold values from -6 to 6
- q_gain: float32 [2560], P('head'), may hold values from 0.25 to 1.75
- k_gain: float32 [2560], P('head'), may hold values from 0.25 to 1.75
- clip_frames: int32 [4, 8], P('clip'), may hold values from 1 to 36, 64 in all within a row
- out_weight: bfloat16 [2560, 5120], P('head', 'clip'), may hold values from -0.125 to 0.125
Outputs:
- attended: bfloat16 [4, 2048, 2560], P('clip', 'seq', 'head')
- projected: bfloat16 [4, 2048, 5120], P('clip', 'seq', 'head')
Inputs may be any that keep to these rules, and one draw needn't show every extreme that they name: `clip_frames`: each row holds 8 lengths summing to 64; the longest is exactly 36.
All inputs are finite; a program needn't handle non-finite values.
Results may differ from a plain program's by a relative error of at most 0.0098.
Values may be sent and summed in bfloat16 or wider, within the bound.
A program may use at most 128 MiB of HBM per device.

v0:
```python
import math

import jax
import jax.numpy as jnp
from jax import lax
from jax.sharding import PartitionSpec as P

HEADS = 20
HEAD_DIM = 128
FR_DEV = 4
TOK_FRAME = 32


def frame_ids(lengths_row, count):
    ends = jnp.cumsum(lengths_row)
    marks = (jnp.arange(count, dtype=jnp.int32)[:, None] >= ends[None, :]).astype(jnp.int32)
    return jnp.sum(marks, axis=1)


def body(queries, keys, values, q_gain, k_gain, clip_frames, out_weight):
    tok_rows = queries.shape[1]
    width = queries.shape[2]
    heads_here = width // HEAD_DIM
    seq_count = lax.axis_size("seq")
    seq_place = lax.axis_index("seq")
    q_float = queries[0].astype(jnp.float32)
    k_float = keys[0].astype(jnp.float32)
    sum_q, sum_k = lax.psum(
        (jnp.sum(q_float * q_float, axis=1), jnp.sum(k_float * k_float, axis=1)), "head"
    )
    q_norm = (q_float * lax.rsqrt(sum_q / (HEADS * HEAD_DIM) + 1e-06)[:, None] * q_gain).astype(
        jnp.bfloat16
    )
    k_norm = (k_float * lax.rsqrt(sum_k / (HEADS * HEAD_DIM) + 1e-06)[:, None] * k_gain).astype(
        jnp.bfloat16
    )
    frame_clip = frame_ids(clip_frames[0], FR_DEV * seq_count)
    token_clip = frame_clip[jnp.arange(tok_rows * seq_count, dtype=jnp.int32) // TOK_FRAME]
    clip_here = lax.dynamic_slice_in_dim(token_clip, seq_place * tok_rows, tok_rows, 0)
    q_heads = q_norm.reshape(tok_rows, heads_here, HEAD_DIM)
    scale = HEAD_DIM ** (-0.5)

    def attend_block(carry, k_block, v_block, ids):
        top, total, summed = carry
        count = k_block.shape[0]
        score = (
            jnp.einsum(
                "qhd,khd->hqk",
                q_heads,
                k_block.reshape(count, heads_here, HEAD_DIM),
                preferred_element_type=jnp.float32,
            )
            * scale
        )
        same = (clip_here[:, None] == ids[None, :])[None]
        score = jnp.where(same, score, jnp.float32(-1e30))
        top_new = jnp.maximum(top, jnp.max(score, axis=-1))
        expo = jnp.where(same, jnp.exp(score - top_new[..., None]), jnp.float32(0.0))
        factor = jnp.exp(top - top_new)
        weights = expo.astype(jnp.bfloat16)
        added = jnp.einsum(
            "hqk,khd->hqd",
            weights,
            v_block.reshape(count, heads_here, HEAD_DIM),
            preferred_element_type=jnp.float32,
        )
        return (
            top_new,
            total * factor + jnp.sum(expo, axis=-1),
            summed * factor[..., None] + added,
        )

    start_state = (
        jnp.full((heads_here, tok_rows), -1e30, jnp.float32),
        jnp.zeros((heads_here, tok_rows), jnp.float32),
        jnp.zeros((heads_here, tok_rows, HEAD_DIM), jnp.float32),
    )
    k_whole, v_whole = (
        lax.all_gather(k_norm[None], "seq", axis=1, tiled=True),
        lax.all_gather(values, "seq", axis=1, tiled=True),
    )
    count = k_whole.shape[1]
    step_rows = math.gcd(count, 1024)
    blocks = count // step_rows
    ids = token_clip

    def advance(state, items):
        return (attend_block(state, items[0], items[1], items[2]), None)

    stacked = (
        k_whole[0].reshape(blocks, step_rows, width),
        v_whole[0].reshape(blocks, step_rows, width),
        ids.reshape(blocks, step_rows),
    )
    top, total, summed = lax.scan(advance, start_state, stacked)[0]
    attended_flat = (
        (summed / total[..., None]).transpose(1, 0, 2).reshape(tok_rows, width).astype(jnp.bfloat16)
    )
    partial_value = jnp.dot(
        attended_flat,
        lax.all_gather(out_weight, "clip", axis=1, tiled=True),
        preferred_element_type=jnp.float32,
    )
    projected = lax.psum_scatter(partial_value, "head", scatter_dimension=1, tiled=True).astype(
        jnp.bfloat16
    )[None]
    return (attended_flat[None], projected)


def solution(mesh):
    in_specs = (
        P("clip", "seq", "head"),
        P("clip", "seq", "head"),
        P("clip", "seq", "head"),
        P("head"),
        P("head"),
        P("clip", None),
        P("head", "clip"),
    )
    out_specs = (P("clip", "seq", "head"), P("clip", "seq", "head"))
    return jax.shard_map(body, mesh=mesh, in_specs=in_specs, out_specs=out_specs, check_vma=False)
```

profile of v0, /device:TPU:1, one launch (start us, length us, event | category | flops | bytes accessed | tf_op | source)
XLA Modules:
  0.0 287.8 jit_solution(9625818479298958156)
XLA Ops:
  9.7 3.5 %all-reduce = (f32[128]{0:T(128)S(1)}, f32[128]{0:T(128)S(1)}) all-reduce(f32[128]{0:T(128)S(1)} %fusion.17, f32[128]{0:T(128)S(1)} %multiply_reduce_fusion), channel_id=1, replica_groups=mesh['seq'=16,'head'=2,'clip'=4] {'head'}, use_global_device_ids=true, to_apply=%region_1.0 | all-reduce | flops 256 | bytes 2048 | tf_op jit(solution)/shard_map/psum | solution.py:28
  13.3 1.8 fusion.19
  22.7 4.5 %compare_select_fusion.1 = s32[2048,1]{0,1:T(1,128)S(1)} fusion(s32[]{:T(128)} %bitcast.59, s32[]{:T(128)} %bitcast.60, s32[]{:T(128)} %bitcast.61, s32[]{:T(128)} %bitcast.62, s32[]{:T(128)} %bitcast.63, s32[]{:T(128)} %bitcast.65, s32[]{:T(128)} %bitcast.64), kind=kLoop, calls=%fused_computation.91 | loop fusion | flops 47104 | bytes 8220 | tf_op jit(solution)/shard_map/gather | solution.py:38
  27.2 36.0 %select_select_fusion = s32[2048]{0:T(1024)S(1)} fusion(pred[2048]{0:T(1024)(128)(4,1)S(1)} %compare_reduce_fusion, pred[2048]{0:T(1024)(128)(4,1)S(1)} %compare_reduce_fusion.1, pred[2048]{0:T(1024)(128)(4,1)S(1)} %compare_reduce_fusion.2, pred[2048]{0:T(1024)(128)(4,1)S(1)} %compare_reduce_fusion.3, pred[2048]{0:T(1024)(128)(4,1)S(1)} %compare_reduce_fusion.4, ...), kind=kLoop, calls=%fused_computation.101 | loop fusion | flops 116736 | bytes 133348 | tf_op jit(solution)/shard_map/gather | solution.py:38
  63.8 10.2 %all-gather.4.cloned.1.call-done = bf16[1,2048,1280]{2,1,0:T(8,128)(2,1)} async-done(((bf16[1,128,1280]{2,1,0:T(8,128)(2,1)}), bf16[1,2048,1280]{2,1,0:T(8,128)(2,1)}) %all-gather.4.cloned.1.call-update) | async-done | bytes 5242896 | tf_op jit(solution)/shard_map/all_gather | solution.py:79
  73.9 58.3 %all-gather.6.cloned.1.call-done = bf16[1,2048,1280]{2,1,0:T(8,128)(2,1)} async-done(((bf16[1,128,1280]{2,1,0:T(8,128)(2,1)}), bf16[1,2048,1280]{2,1,0:T(8,128)(2,1)}) %all-gather.6.cloned.1.call-update) | async-done | bytes 5242896 | tf_op jit(solution)/shard_map/all_gather | solution.py:80
  132.2 51.2 %while.15 = (s32[]{:T(128)}, f32[10,128]{1,0:T(8,128)S(1)}, f32[10,128]{1,0:T(8,128)S(1)}, f32[10,128,128]{2,1,0:T(8,128)}, s32[128]{0:T(128)S(1)}, /*index=5*/s...) while((s32[]{:T(128)}, f32[10,128]{1,0:T(8,128)S(1)}, ...), condition=%wide.region_9.10_spmd.clone, body=%wide.region_6.9_spmd.clone.sunk | while | flops 688756992 | bytes 54686360 | solution.py:95
  132.4 5.2 %constant_dynamic-slice_fusion.6 = (bf16[1,1024,1280]{2,1,0:T(8,128)(2,1)}, bf16[1,1024,1280]{2,1,0:T(8,128)(2,1)}) fusion(bf16[2,1024,1280]{2,1,0:T(8,128)(2,1)} %get-tuple-element.302, s32[]{:T(128)} %get-tuple-element.283, bf16[2,1024,1280]{2,1,0:T(8,128)(2,1)} %get-tuple-element.300), kind=kLoop, calls=%fused_computation.18.clone.1 | loop fusion | bytes 10485764 | tf_op jit(solution)/shard_map/while/body/jit(dynamic_index_in_dim)/dynamic_slice | solution.py:95
  137.6 3.0 %copy.43 = bf16[1,1024,1280]{1,2,0:T(8,128)(2,1)S(1)} copy(bf16[1,1024,1280]{2,1,0:T(8,128)(2,1)} %get-tuple-element.266) | data formatting | bytes 5242880 | tf_op jit(solution)/shard_map/while/body/jit(dynamic_index_in_dim)/dynamic_slice | solution.py:95
  140.6 3.9 %fusion.42 = (f32[10,128]{1,0:T(8,128)S(1)}, f32[10,1024,128]{2,1,0:T(8,128)}) fusion(pred[128,1024]{0,1:T(8,128)(4,1)S(1)} %broadcast_compare_fusion.2, bf16[1024,10,128]{0,2,1:T(8,128)(2,1)S(1)} %bitcast.118, bf16[128,10,128]{2,0,1:T(8,128)(2,1)S(1)} %get-tuple-element.301), kind=kOutput, calls=%fused_computation.2.clone.1 | convolution fusion | flops 339475200 | bytes 8328192 | tf_op jit(solution)/shard_map/while/body/eval_jaxpr/qhd,khd->hqk/dot_general | solution.py:47
  144.5 4.7 %fusion.43 = f32[10,128]{1,0:T(8,128)S(1)} fusion(f32[10,1024,128]{2,1,0:T(8,128)} %get-tuple-element.268, f32[10,128]{1,0:T(8,128)S(1)} %select_maximum_fusion.2, pred[128,1024]{0,1:T(8,128)(4,1)S(1)} %broadcast_compare_fusion.2), kind=kLoop, calls=%fused_computation.4.clone.1 | loop fusion | flops 6552320 | bytes 5384192 | tf_op jit(solution)/shard_map/while/body/eval_jaxpr/reduce_sum | solution.py:69
  149.3 2.7 copy.44
  152.0 6.2 %fusion.45 = f32[10,128,128]{2,1,0:T(8,128)} fusion(bf16[1024,10,128]{0,2,1:T(8,128)(2,1)} %bitcast.119, f32[10,1024,128]{2,1,0:T(8,128)} %get-tuple-element.268, f32[10,128]{1,0:T(8,128)S(1)} %select_maximum_fusion.2, pred[128,1024]{0,1:T(8,128)(4,1)S(1)} %broadcast_compare_fusion.2, f32[10,128,128]{2,1,0:T(8,128)} %get-tuple-element.286, ...), kind=kOutput, calls=%fused_computation.11.clone.1 | convolution fusion | flops 342589440 | bytes 9316353 | tf_op jit(solution)/shard_map/while/body/eval_jaxpr/hqk,khd->hqd/dot_general | solution.py:61
  158.4 5.3 %constant_dynamic-slice_fusion.6 = (bf16[1,1024,1280]{2,1,0:T(8,128)(2,1)}, bf16[1,1024,1280]{2,1,0:T(8,128)(2,1)}) fusion(bf16[2,1024,1280]{2,1,0:T(8,128)(2,1)} %get-tuple-element.302, s32[]{:T(128)} %get-tuple-element.283, bf16[2,1024,1280]{2,1,0:T(8,128)(2,1)} %get-tuple-element.300), kind=kLoop, calls=%fused_computation.18.clone.1 | loop fusion | bytes 10485764 | tf_op jit(solution)/shard_map/while/body/jit(dynamic_index_in_dim)/dynamic_slice | solution.py:95
  163.7 3.0 %copy.43 = bf16[1,1024,1280]{1,2,0:T(8,128)(2,1)S(1)} copy(bf16[1,1024,1280]{2,1,0:T(8,128)(2,1)} %get-tuple-element.266) | data formatting | bytes 5242880 | tf_op jit(solution)/shard_map/while/body/jit(dynamic_index_in_dim)/dynamic_slice | solution.py:95
  166.8 3.6 %fusion.42 = (f32[10,128]{1,0:T(8,128)S(1)}, f32[10,1024,128]{2,1,0:T(8,128)}) fusion(pred[128,1024]{0,1:T(8,128)(4,1)S(1)} %broadcast_compare_fusion.2, bf16[1024,10,128]{0,2,1:T(8,128)(2,1)S(1)} %bitcast.118, bf16[128,10,128]{2,0,1:T(8,128)(2,1)S(1)} %get-tuple-element.301), kind=kOutput, calls=%fused_computation.2.clone.1 | convolution fusion | flops 339475200 | bytes 8328192 | tf_op jit(solution)/shard_map/while/body/eval_jaxpr/qhd,khd->hqk/dot_general | solution.py:47
  170.4 4.0 %fusion.43 = f32[10,128]{1,0:T(8,128)S(1)} fusion(f32[10,1024,128]{2,1,0:T(8,128)} %get-tuple-element.268, f32[10,128]{1,0:T(8,128)S(1)} %select_maximum_fusion.2, pred[128,1024]{0,1:T(8,128)(4,1)S(1)} %broadcast_compare_fusion.2), kind=kLoop, calls=%fused_computation.4.clone.1 | loop fusion | flops 6552320 | bytes 5384192 | tf_op jit(solution)/shard_map/while/body/eval_jaxpr/reduce_sum | solution.py:69
  174.4 2.7 copy.44
  177.1 6.3 %fusion.45 = f32[10,128,128]{2,1,0:T(8,128)} fusion(bf16[1024,10,128]{0,2,1:T(8,128)(2,1)} %bitcast.119, f32[10,1024,128]{2,1,0:T(8,128)} %get-tuple-element.268, f32[10,128]{1,0:T(8,128)S(1)} %select_maximum_fusion.2, pred[128,1024]{0,1:T(8,128)(4,1)S(1)} %broadcast_compare_fusion.2, f32[10,128,128]{2,1,0:T(8,128)} %get-tuple-element.286, ...), kind=kOutput, calls=%fused_computation.11.clone.1 | convolution fusion | flops 342589440 | bytes 9316353 | tf_op jit(solution)/shard_map/while/body/eval_jaxpr/hqk,khd->hqd/dot_general | solution.py:61
  183.4 1.3 copy.34
  184.8 71.7 %all-gather.8.cloned.1.call-done = bf16[1280,5120]{1,0:T(8,128)(2,1)} async-done(((bf16[1280,1280]{1,0:T(8,128)(2,1)}), bf16[1280,5120]{1,0:T(8,128)(2,1)}) %all-gather.8.cloned.1.call-update) | async-done | bytes 13107216 | tf_op jit(solution)/shard_map/all_gather | solution.py:101
  256.5 8.1 %fusion.24 = f32[128,5120]{1,0:T(8,128)} fusion(bf16[128,1280]{0,1:T(8,128)(2,1)S(1)} %bitcast.122, bf16[1280,5120]{1,0:T(8,128)(2,1)} %all-gather.8.cloned.1.call-done), kind=kOutput, calls=%fused_computation.110 | convolution fusion | flops 1677721600 | bytes 16056320 | tf_op jit(solution)/shard_map/dot_general | solution.py:99
  265.5 13.6 %reduce-scatter.2.cloned.1.call-done = f32[128,2560]{1,0:T(8,128)} async-done(((f32[128,5120]{1,0:T(8,128)}), f32[128,2560]{1,0:T(8,128)}) %reduce-scatter.2.cloned.1.call-update) | async-done | bytes 1310736 | tf_op jit(solution)/shard_map/reduce_scatter | solution.py:104
  279.1 2.2 convert_bitcast_fusion
  (103 shorter events, 12.0 us)
Async XLA Ops:
  7.2 9.6 %copy-start.2 = (s32[1,8]{1,0:T(1,128)S(1)}, s32[1,8]{1,0:T(1,128)}, u32[]{:S(2)}) copy-start(s32[1,8]{1,0:T(1,128)} %param.14) | copy-start | bytes 100
  7.2 56.1 %copy-start.1 = (f32[1280]{0:T(1024)S(1)}, f32[1280]{0:T(1024)}, u32[]{:S(2)}) copy-start(f32[1280]{0:T(1024)} %param.12) | copy-start | bytes 15364
  7.2 66.8 %all-gather.4.cloned.1.call-start = ((), (), s32[]{:S(2)}) async-start(), calls=%async_computation.1 | async-start | bytes 5570560 | tf_op jit(solution)/shard_map/all_gather | solution.py:79
  15.1 117.0 %all-gather.6.cloned.1.call-start = ((), (), s32[]{:S(2)}) async-start(), calls=%async_computation.2 | async-start | bytes 5570560 | tf_op jit(solution)/shard_map/all_gather | solution.py:80
  15.9 240.6 %all-gather.8.cloned.1.call-start = ((), (), s32[]{:S(2)}) async-start(), calls=%async_computation.3 | async-start | bytes 16384000 | tf_op jit(solution)/shard_map/all_gather | solution.py:101
  16.6 262.4 %reduce-scatter.2.cloned.1.call-start = ((), (), s32[]{:S(2)}) async-start(), calls=%async_computation.4 | async-start | bytes 3932160 | tf_op jit(solution)/shard_map/reduce_scatter | solution.py:104
  144.5 4.7 %copy-start = (bf16[1,1024,1280]{2,1,0:T(8,128)(2,1)S(1)}, bf16[1,1024,1280]{2,1,0:T(8,128)(2,1)}, u32[]{:S(2)}) copy-start(bf16[1,1024,1280]{2,1,0:T(8,128)(2,1)} %get-tuple-element.270) | copy-start | bytes 7864324 | tf_op jit(solution)/shard_map/while
  170.4 4.0 %copy-start = (bf16[1,1024,1280]{2,1,0:T(8,128)(2,1)S(1)}, bf16[1,1024,1280]{2,1,0:T(8,128)(2,1)}, u32[]{:S(2)}) copy-start(bf16[1,1024,1280]{2,1,0:T(8,128)(2,1)} %get-tuple-element.270) | copy-start | bytes 7864324 | tf_op jit(solution)/shard_map/while
Sparse Core Ops, SparseCore 0:
  15.3 58.6 all-gather.3
  76.1 56.0 all-gather.5
  133.9 122.5 all-gather.7
  264.7 14.3 reduce-scatter.1
where the time goes:
time: 289 us; the launch traced here: 288 us
  waiting for transfers between devices  155 us (54%)
  other arithmetic  58.4 us (20%)
  local copies, waits for them, and re-layouts  28.6 us (10%)
  matrix products  28.1 us (10%)
  between operations  13.9 us (5%)
  blocking collectives  3.54 us (1%)
    all_gather x1, waiting for transfers between devices, body(): lax.all_gather(out_weight, 'clip', axis=1, tiled=True)  71.7 us
    all_gather x1, waiting for transfers between devices, body(): lax.all_gather(values, 'seq', axis=1, tiled=True)  58.3 us
    gather x59, other arithmetic, body(): frame_clip[jnp.arange(tok_rows * seq_count, dtype=jnp.int32) // TOK_FRAME]  43.3 us
    dynamic_slice x8, local copies, waits for them, and re-layouts, body(): top, total, summed = lax.scan(advance, start_state, stacked)[0]  22 us
    reduce_scatter x1, waiting for transfers between devices, body(): lax.psum_scatter(partial_value, 'head', scatter_dimension=1, tiled=True)  13.6 us
    dot_general x2, matrix products, attend_block(): jnp.einsum('hqk,khd->hqd', weights, v_block.reshape(count, heads_here, HE...  12.5 us
    all_gather x1, waiting for transfers between devices, body(): lax.all_gather(k_norm[None], 'seq', axis=1, tiled=True)  10.2 us
    reduce_sum x2, other arithmetic, attend_block(): jnp.sum(expo, axis=-1)  8.68 us
  transfers between devices with their start and end apart: 4, of which 4 were waited for; matrix products, arithmetic and copies ran while one was open for 35% of the time, Pallas kernels for 0%

commit v1 on v0

v1 whole, which is shorter than its diff:
```python
import jax
import jax.numpy as jnp
from jax import lax
from jax.experimental import pallas as pl
from jax.experimental.pallas import tpu as pltpu
from jax.sharding import PartitionSpec as P

HEADS = 20
HEAD_DIM = 128
HD = HEADS * HEAD_DIM
TOK_FRAME = 32
CLIPS = 8
SEQ = 16
ROWS = 128
WIDE = 1280
HERE = WIDE // HEAD_DIM
CHUNKS = 4
TOKENS = SEQ * ROWS
OUT_HALF = 640
MASKED = -1e30
MESH = pl.DeviceIdType.MESH


def lanes(start, size=HEAD_DIM):
    return pl.ds(pl.multiple_of(start, 128), size)


def rows(start, size):
    return pl.ds(pl.multiple_of(start, 32), size)


def owner_of(core, head):
    turn = head // 4
    z = head % 4 + 2 * core * (head // 8)
    y = (z + turn * (1 + 2 * core)) % 4
    return z * 4 + y


def owned_by(core, place):
    z, y = place // 4, place % 4
    off = (y - z + 4) % 4
    turn = jnp.where(off == 0, 0, jnp.where(off == 2, 2, jnp.where(off == 1 + 2 * core, 1, -1)))
    last = z - 2 * core
    head = jnp.where(turn == 2, 8 + last, turn * 4 + z)
    good = (turn >= 0) & ((turn < 2) | ((last >= 0) & (last < 2)))
    return jnp.where(good, head, -1)


def kernel(
    lens, q_in, k_in, v_in, q_gain, k_gain, w_in, att_out, proj_out,
    qf, kf, qn, kn, sums, qx, kx, vx, back, ag, w2, res,
    load_sem, sum_sem, w_sem, v_sem, k_sem, q_sem, r_sem, x_sem, d_sem, o_sem, a_sem,
    s_sum, s_w, s_v, s_k, s_q, s_r, s_x, s_d, s_o,
):
    place, core, group = lax.axis_index("seq"), lax.axis_index("head"), lax.axis_index("clip")
    other = 1 - core
    mine = owned_by(core, place)
    owner = mine >= 0

    loads = [
        pltpu.make_async_copy(q_in.at[0], qf, load_sem.at[0]),
        pltpu.make_async_copy(k_in.at[0], kf, load_sem.at[1]),
        pltpu.make_async_copy(w_in.at[:, lanes(core * OUT_HALF, OUT_HALF)], w2.at[core], load_sem.at[2]),
    ]
    for load in loads:
        load.start()

    barrier = pltpu.get_barrier_semaphore()

    def greet_plane(i, carry):
        to = (place + i) % SEQ
        pl.semaphore_signal(barrier, inc=1, device_id=(to, core, group), device_id_type=MESH)
        return carry

    lax.fori_loop(1, SEQ, greet_plane, 0)
    pl.semaphore_signal(barrier, inc=1, device_id=(place, other, group), device_id_type=MESH)

    def greet_line(i, carry):
        to = (group + i) % 4
        pl.semaphore_signal(barrier, inc=1, device_id=(place, core, to), device_id_type=MESH)
        pl.semaphore_signal(barrier, inc=1, device_id=(place, other, to), device_id_type=MESH)
        return carry

    lax.fori_loop(1, 4, greet_line, 0)
    pl.semaphore_wait(barrier, SEQ - 1 + 1 + 6)

    def to_owners(copies):
        def one(i, carry):
            head = (i + place) % HERE
            to = owner_of(core, head)

            @pl.when(to == place)
            def _():
                for src, dst, send, recv in copies(head):
                    pltpu.make_async_copy(src, dst, recv).start()

            @pl.when(to != place)
            def _():
                for src, dst, send, recv in copies(head):
                    pltpu.make_async_remote_copy(
                        src, dst, send, recv, device_id=(to, core, group), device_id_type=MESH
                    ).start()

            return carry

        lax.fori_loop(0, HERE, one, 0)

    own_rows = rows(place * ROWS, ROWS)
    to_owners(lambda head: [(v_in.at[0, :, lanes(head * 128)], vx.at[own_rows, pl.ds(0, 128)], s_v, v_sem)])

    loads[0].wait()
    loads[1].wait()
    q_float = qf[...].astype(jnp.float32)
    k_float = kf[...].astype(jnp.float32)
    sum_q = jnp.sum(q_float * q_float, axis=1, keepdims=True)
    sum_k = jnp.sum(k_float * k_float, axis=1, keepdims=True)
    low = lax.broadcasted_iota(jnp.int32, (ROWS, 128), 1) < 64
    sums[0] = jnp.where(low, sum_q, sum_k)
    give_sums = pltpu.make_async_remote_copy(
        sums.at[0], sums.at[1], s_sum, sum_sem, device_id=(place, other, group), device_id_type=MESH
    )
    give_sums.start()
    give_w = pltpu.make_async_remote_copy(
        w_in.at[:, lanes(other * OUT_HALF, OUT_HALF)], w2.at[core], s_w, w_sem,
        device_id=(place, other, group), device_id_type=MESH,
    )
    give_w.start()
    give_sums.wait()
    both = sums[0] + sums[1]
    k_rate = lax.rsqrt(both[:, 64:65] / HD + 1e-06)
    kn[...] = (kf[...].astype(jnp.float32) * k_rate * k_gain[...]).astype(jnp.bfloat16)
    to_owners(lambda head: [(kn.at[:, lanes(head * 128)], kx.at[own_rows, pl.ds(0, 128)], s_k, k_sem)])
    q_rate = lax.rsqrt(both[:, 0:1] / HD + 1e-06)
    qn[...] = (qf[...].astype(jnp.float32) * q_rate * q_gain[...]).astype(jnp.bfloat16)

    def send_q(chunk, carry):
        to_owners(
            lambda head: [
                (
                    qn.at[rows(chunk * 32, 32), lanes(head * 128)],
                    qx.at[chunk, rows(place * 32, 32), pl.ds(0, 128)],
                    s_q,
                    q_sem.at[chunk],
                )
            ]
        )
        return carry

    lax.fori_loop(0, CHUNKS, send_q, 0)

    @pl.when(owner)
    def _():
        lane = lax.broadcasted_iota(jnp.int32, (1, 128), 1)
        first = jnp.zeros((1, 128), jnp.int32)
        last = jnp.zeros((1, 128), jnp.int32)
        end = jnp.int32(0)
        for clip in range(CLIPS):
            first = jnp.where(lane == clip, end, first)
            end = end + lens[0, clip]
            last = jnp.where(lane == clip, end, last)
        one = jnp.ones((), jnp.float32)
        zero = jnp.zeros((), jnp.float32)
        frame = lax.broadcasted_iota(jnp.int32, (TOKENS, 128), 0) // TOK_FRAME
        kx[:, 128:256] = jnp.where((frame >= first) & (frame < last), one, zero).astype(jnp.bfloat16)
        vx[:, 128:256] = jnp.ones((TOKENS, 128), jnp.bfloat16)
        for chunk in range(CHUNKS):
            frame = lax.broadcasted_iota(jnp.int32, (SEQ * 32, 128), 0) // 32 * CHUNKS + chunk
            off = jnp.logical_not((frame >= first) & (frame < last)) & (lane < CLIPS)
            qx[chunk, :, 128:256] = jnp.where(off, MASKED * one, zero).astype(jnp.bfloat16)
        pltpu.make_async_copy(vx.at[:, pl.ds(0, 128)], vx.at[:, pl.ds(0, 128)], v_sem).wait()
        pltpu.make_async_copy(kx.at[:, pl.ds(0, 128)], kx.at[:, pl.ds(0, 128)], k_sem).wait()

    loads[2].wait()
    give_w.wait()
    factor = HEAD_DIM ** (-0.5) * 1.4426950408889634

    def step(t, carry):
        @pl.when(owner & (t < CHUNKS))
        def _():
            chunk = t
            pltpu.make_async_copy(
                qx.at[chunk, :, pl.ds(0, 128)], qx.at[chunk, :, pl.ds(0, 128)], q_sem.at[chunk]
            ).wait()

            def attend(part, carry):
                span = rows(part * 256, 256)
                score = lax.dot_general(
                    qx[chunk, span, :], kx[...], (((1,), (1,)), ((), ())), preferred_element_type=jnp.float32
                )
                top = jnp.max(score, axis=1, keepdims=True)
                weights = jnp.exp2((score - top) * factor).astype(jnp.bfloat16)
                summed = jnp.dot(weights, vx[...], preferred_element_type=jnp.float32)
                back[chunk, span, :] = (summed[:, :128] / summed[:, 128:]).astype(jnp.bfloat16)
                return carry

            lax.fori_loop(0, 2, attend, 0)

            def give(i, carry):
                to = (place + i) % SEQ
                src = back.at[chunk, rows(to * 32, 32)]
                dst = ag.at[chunk, core, rows(group * 32, 32), lanes(mine * 128)]

                @pl.when(i == 0)
                def _():
                    pltpu.make_async_copy(src, dst, r_sem.at[chunk]).start()

                @pl.when(i > 0)
                def _():
                    pltpu.make_async_remote_copy(
                        src, dst, s_r, r_sem.at[chunk], device_id=(to, core, group), device_id_type=MESH
                    ).start()

                return carry

            lax.fori_loop(0, SEQ, give, 0)

        @pl.when((t >= 1) & (t < CHUNKS + 1))
        def _():
            chunk = t - 1
            block = ag.at[chunk, core, rows(group * 32, 32)]
            pltpu.make_async_copy(block, block, r_sem.at[chunk]).wait()
            for i in range(1, 4):
                pltpu.make_async_remote_copy(
                    block, block, s_x, x_sem.at[chunk],
                    device_id=(place, core, (group + i) % 4), device_id_type=MESH,
                ).start()
            pltpu.make_async_remote_copy(
                block, block, s_d, d_sem.at[chunk], device_id=(place, other, group), device_id_type=MESH
            ).start()
            pltpu.make_async_copy(block, att_out.at[0, rows(chunk * 32, 32)], a_sem).start()

        @pl.when((t >= 2) & (t < CHUNKS + 2))
        def _():
            chunk = t - 2
            three = ag.at[chunk, core, pl.ds(0, 96)]
            pltpu.make_async_copy(three, three, x_sem.at[chunk]).wait()
            for i in range(1, 4):
                block = ag.at[chunk, core, rows((group + i) % 4 * 32, 32)]
                pltpu.make_async_remote_copy(
                    block, block, s_d, d_sem.at[chunk], device_id=(place, other, group), device_id_type=MESH
                ).start()

        @pl.when(t >= 3)
        def _():
            chunk = t - 3
            half = ag.at[chunk, other]
            pltpu.make_async_copy(half, half, d_sem.at[chunk]).wait()
            total = jnp.dot(ag[chunk, 0], w2[0], preferred_element_type=jnp.float32)
            total += jnp.dot(ag[chunk, 1], w2[1], preferred_element_type=jnp.float32)
            res[chunk] = total.astype(jnp.bfloat16)
            to_core = group // 2
            dst = proj_out.at[0, rows(chunk * 32, 32), lanes((group % 2) * WIDE + core * OUT_HALF, OUT_HALF)]
            for i in range(4):
                to = (group + i) % 4
                src = res.at[chunk, rows(to * 32, 32)]

                def far(src=src, to=to):
                    pltpu.make_async_remote_copy(
                        src, dst, s_o, o_sem, device_id=(place, to_core, to), device_id_type=MESH
                    ).start()

                if i:
                    far()
                else:
                    pl.when(to_core != core)(far)

                    @pl.when(to_core == core)
                    def _(src=src):
                        pltpu.make_async_copy(src, dst, o_sem).start()

        return carry

    lax.fori_loop(0, CHUNKS + 3, step, 0)

    def done(ref, sem):
        pltpu.make_async_copy(ref, ref, sem).wait()

    @pl.when(owner)
    def _():
        for sem in (s_v, s_k, s_q):
            done(kn.at[:, pl.ds(0, 9 * 128)], sem)
        done(kx.at[pl.ds(0, TOKENS - ROWS), pl.ds(0, 128)], s_r)

    @pl.when(jnp.logical_not(owner))
    def _():
        for sem in (s_v, s_k, s_q):
            done(kn, sem)

    done(ag.at[pl.ds(0, 3), 0], s_x)
    done(ag.at[:, 0], s_d)

    @pl.when(group // 2 == core)
    def _():
        done(res.at[pl.ds(0, 3)], s_o)

    @pl.when(group // 2 != core)
    def _():
        done(res, s_o)

    done(att_out, a_sem)
    done(proj_out, o_sem)


def body(queries, keys, values, q_gain, k_gain, clip_frames, out_weight):
    anywhere = pl.BlockSpec(memory_space=pl.ANY)
    vmem = pl.BlockSpec(memory_space=pltpu.VMEM)
    bf16, f32 = jnp.bfloat16, jnp.float32
    dma = pltpu.SemaphoreType.DMA
    return pl.pallas_call(
        kernel,
        out_shape=(
            jax.ShapeDtypeStruct((1, ROWS, WIDE), bf16),
            jax.ShapeDtypeStruct((1, ROWS, 2 * WIDE), bf16),
        ),
        in_specs=[pl.BlockSpec(memory_space=pltpu.SMEM), anywhere, anywhere, anywhere, vmem, vmem, anywhere],
        out_specs=(anywhere, anywhere),
        scratch_shapes=[
            pltpu.VMEM((ROWS, WIDE), bf16),
            pltpu.VMEM((ROWS, WIDE), bf16),
            pltpu.VMEM((ROWS, WIDE), bf16),
            pltpu.VMEM((ROWS, WIDE), bf16),
            pltpu.VMEM((2, ROWS, 128), f32),
            pltpu.VMEM((CHUNKS, SEQ * 32, 256), bf16),
            pltpu.VMEM((TOKENS, 256), bf16),
            pltpu.VMEM((TOKENS, 256), bf16),
            pltpu.VMEM((CHUNKS, SEQ * 32, 128), bf16),
            pltpu.VMEM((CHUNKS, 2, 128, WIDE), bf16),
            pltpu.VMEM((2, WIDE, OUT_HALF), bf16),
            pltpu.VMEM((CHUNKS, 128, OUT_HALF), bf16),
            dma((3,)), dma, dma, dma, dma, dma((CHUNKS,)), dma((CHUNKS,)), dma((CHUNKS,)), dma((CHUNKS,)), dma, dma,
            dma, dma, dma, dma, dma, dma, dma, dma, dma,
        ],
        compiler_params=pltpu.CompilerParams(
            collective_id=0, has_side_effects=True, vmem_limit_bytes=56 << 20
        ),
        cost_estimate=pl.CostEstimate(flops=3 * 10**9, bytes_accessed=8 << 20, transcendentals=4 << 20),
    )(clip_frames, queries, keys, values, q_gain[None], k_gain[None], out_weight)


def solution(mesh):
    in_specs = (
        P("clip", "seq", "head"),
        P("clip", "seq", "head"),
        P("clip", "seq", "head"),
        P("head"),
        P("head"),
        P("clip", None),
        P("head", "clip"),
    )
    out_specs = (P("clip", "seq", "head"), P("clip", "seq", "head"))
    return jax.shard_map(body, mesh=mesh, in_specs=in_specs, out_specs=out_specs, check_vma=False)
```

time: 289 us -> 69.2 us (0.24)
  waiting for transfers between devices: 155 us -> 0 us
  Pallas kernels: 0 us -> 61.9 us
  other arithmetic: 58.4 us -> 0 us
  matrix products: 28.1 us -> 0 us
  local copies, waits for them, and re-layouts: 28.6 us -> 6.27 us
  between operations: 13.9 us -> 0.64 us
  blocking collectives: 3.54 us -> 0 us
    all_gather x3 -> x0, waiting for transfers between devices: 140 us -> none  [the longest x1 71.7 us: body(): lax.all_gather(out_weight, 'clip', axis=1, tiled=True)]
    pallas_call x0 -> x1, Pallas kernels: none -> 61.9 us  [body(): pl.pallas_call(kernel, out_shape=(jax.ShapeDtypeStruct((1, ROWS, WIDE), b...]
    gather x59 -> x0, other arithmetic: 43.3 us -> none  [body(): frame_clip[jnp.arange(tok_rows * seq_count, dtype=jnp.int32) // TOK_FRAME]]
    dot_general x5 -> x0, matrix products: 28.1 us -> none  [the longest x2 12.5 us: attend_block(): jnp.einsum('hqk,khd->hqd', weights, v_block.reshape(count, heads_here, HE...]
    dynamic_slice x9 -> x0, local copies, waits for them, and re-layouts: 22.1 us -> none  [the longest x8 22 us: body(): top, total, summed = lax.scan(advance, start_state, stacked)[0]]
    reduce_scatter x1 -> x0, waiting for transfers between devices: 13.6 us -> none  [body(): lax.psum_scatter(partial_value, 'head', scatter_dimension=1, tiled=True)]
    reduce_sum x5 -> x0, other arithmetic: 10.1 us -> none  [the longest x2 8.68 us: attend_block(): jnp.sum(expo, axis=-1)]
    psum x1 -> x0, blocking collectives: 3.54 us -> none  [body(): lax.psum((jnp.sum(q_float * q_float, axis=1), jnp.sum(k_float * k_float,...]
  transfers between devices with their start and end apart: 4 -> 0, of which waited for: 4 -> 0; matrix products, arithmetic and copies ran while one was open for 35% -> 0% of each run, Pallas kernels for 0% -> 0%
where the time goes in v1:
time: 69.2 us; the launch traced here: 68.8 us
  Pallas kernels  61.9 us (89%)
  local copies, waits for them, and re-layouts  6.27 us (9%)
    pallas_call x1, Pallas kernels, body(): pl.pallas_call(kernel, out_shape=(jax.ShapeDtypeStruct((1, ROWS, WIDE), b...  61.9 us
    unnamed x2, local copies, waits for them, and re-layouts  3.68 us

profile of v1, /device:TPU:1, one launch (start us, length us, event | category | flops | bytes accessed | tf_op | source)
XLA Modules:
  0.0 68.8 jit_solution(5453511651030846149)
XLA Ops:
  0.6 1.3 %broadcast_in_dim.6.q_gain = f32[1,1280]{1,0:T(1,128)} reshape(f32[1280]{0:T(1024)} %param.10) | data formatting | bytes 10240 | tf_op jit(solution)/shard_map/broadcast_in_dim | solution.py:337
  1.9 1.3 %broadcast_in_dim.7.k_gain = f32[1,1280]{1,0:T(1,128)} reshape(f32[1280]{0:T(1024)} %param.11) | data formatting | bytes 10240 | tf_op jit(solution)/shard_map/broadcast_in_dim | solution.py:337
  3.2 61.9 %shard_map.86 = (bf16[1,128,1280]{2,1,0:T(8,128)(2,1)}, bf16[1,128,2560]{2,1,0:T(8,128)(2,1)}) custom-call(s32[1,8]{1,0:T(1,128)} %lens.1, bf16[1,128,1280]{2,1,0:T(8,128)(2,1)} %q_in.1, bf16[1,128,1280]{2,1,0:T(8,128)(2,1)} %k_in.1, bf16[1,128,1280]{2,1,0:T(8,128)(2,1)} %v_in.1, f32[1,1280]{1,0:T(1,128)} %broadcast_in_dim.6.q_gain, ...), custom_call_target="tpu_custom_call" | custom-call | flops 3000000000 | bytes 8388608 | tf_op jit(solution)/shard_map/pallas_call | solution.py:309
  65.2 1.7 %copy.11 = bf16[1,128,1280]{2,1,0:T(8,128)(2,1)} copy(bf16[1,128,1280]{2,1,0:T(8,128)(2,1)} %get-tuple-element.4) | data formatting | bytes 655360
  66.9 2.0 %copy.12 = bf16[1,128,2560]{2,1,0:T(8,128)(2,1)} copy(bf16[1,128,2560]{2,1,0:T(8,128)(2,1)} %get-tuple-element.5) | data formatting | bytes 1310720

commit v2 on v1

v2 whole, which is shorter than its diff:
```python
import jax
import jax.numpy as jnp
from jax import lax
from jax.experimental import pallas as pl
from jax.experimental.pallas import tpu as pltpu
from jax.sharding import PartitionSpec as P

HEADS = 20
HEAD_DIM = 128
HD = HEADS * HEAD_DIM
TOK_FRAME = 32
CLIPS = 8
SEQ = 16
ROWS = 128
WIDE = 1280
HERE = WIDE // HEAD_DIM
PART = 16
CHUNKS = ROWS // PART
SLOTS = CHUNKS // 2
BLOCK = SEQ * PART
KEYS = 512
TOKENS = SEQ * ROWS
LAG_HOME, LAG_LINE, LAG_OUT = 3, 6, 11
MASKED = -1e30
MESH = pl.DeviceIdType.MESH


def lanes(start, size=HEAD_DIM):
    return pl.ds(pl.multiple_of(start, 128), size)


def rows(start, size):
    return pl.ds(pl.multiple_of(start, 16), size)


def owner_of(core, head):
    turn = head // 4
    z = head % 4 + 2 * core * (head // 8)
    y = (z + turn * (1 + 2 * core)) % 4
    return z * 4 + y


def owned_by(core, place):
    z, y = place // 4, place % 4
    off = (y - z + 4) % 4
    turn = jnp.where(off == 0, 0, jnp.where(off == 2, 2, jnp.where(off == 1 + 2 * core, 1, -1)))
    last = z - 2 * core
    head = jnp.where(turn == 2, 8 + last, turn * 4 + z)
    good = (turn >= 0) & ((turn < 2) | ((last >= 0) & (last < 2)))
    return jnp.where(good, head, -1)


def kernel(
    lens, q_in, k_in, v_in, q_gain, k_gain, w_in, att_out, proj_out,
    qf, kf, qn, kn, sums, qx, kx, vx, back, ag, w2, res,
    load_sem, sum_sem, w_sem, v_sem, k_sem, q_sem, r_sem, left_sem, right_sem, far_sem, o_sem, a_sem,
    s_sum, s_w, s_v, s_k, s_q, s_r, s_x, s_f, s_o, s_a,
):
    place, core, group = lax.axis_index("seq"), lax.axis_index("head"), lax.axis_index("clip")
    other = 1 - core
    mine = owned_by(core, place)
    owner = mine >= 0

    loads = [
        pltpu.make_async_copy(q_in.at[0], qf, load_sem.at[0]),
        pltpu.make_async_copy(k_in.at[0], kf, load_sem.at[1]),
        pltpu.make_async_copy(w_in, w2.at[rows(core * WIDE, WIDE)], load_sem.at[2]),
    ]
    for load in loads:
        load.start()

    barrier = pltpu.get_barrier_semaphore()

    def greet_plane(i, carry):
        to = (place + i) % SEQ
        pl.semaphore_signal(barrier, inc=1, device_id=(to, core, group), device_id_type=MESH)
        return carry

    lax.fori_loop(1, SEQ, greet_plane, 0)
    pl.semaphore_signal(barrier, inc=1, device_id=(place, other, group), device_id_type=MESH)

    left, right = (group + 3) % 4, (group + 1) % 4
    for to in (left, right):
        pl.semaphore_signal(barrier, inc=1, device_id=(place, core, to), device_id_type=MESH)
    loads[0].wait()
    loads[1].wait()
    q_float = qf[...].astype(jnp.float32)
    k_float = kf[...].astype(jnp.float32)
    sum_q = jnp.sum(q_float * q_float, axis=1, keepdims=True)
    sum_k = jnp.sum(k_float * k_float, axis=1, keepdims=True)
    low = lax.broadcasted_iota(jnp.int32, (ROWS, 128), 1) < 64
    sums[0] = jnp.where(low, sum_q, sum_k)
    pl.semaphore_wait(barrier, SEQ - 1 + 1 + 2)

    def to_owners(copies):
        def one(i, carry):
            head = (i + place) % HERE
            to = owner_of(core, head)

            @pl.when(to == place)
            def _():
                for src, dst, send, recv in copies(head):
                    pltpu.make_async_copy(src, dst, recv).start()

            @pl.when(to != place)
            def _():
                for src, dst, send, recv in copies(head):
                    pltpu.make_async_remote_copy(
                        src, dst, send, recv, device_id=(to, core, group), device_id_type=MESH
                    ).start()

            return carry

        lax.fori_loop(0, HERE, one, 0)

    own_rows = rows(place * ROWS, ROWS)
    to_owners(lambda head: [(v_in.at[0, :, lanes(head * 128)], vx.at[own_rows, pl.ds(0, 128)], s_v, v_sem)])

    give_sums = pltpu.make_async_remote_copy(
        sums.at[0], sums.at[1], s_sum, sum_sem, device_id=(place, other, group), device_id_type=MESH
    )
    give_sums.start()
    give_w = pltpu.make_async_remote_copy(
        w_in, w2.at[rows(core * WIDE, WIDE)], s_w, w_sem,
        device_id=(place, other, group), device_id_type=MESH,
    )
    give_w.start()
    give_sums.wait()
    both = sums[0] + sums[1]
    k_rate = lax.rsqrt(both[:, 64:65] / HD + 1e-06)
    kn[...] = (kf[...].astype(jnp.float32) * k_rate * k_gain[...].reshape(1, WIDE)).astype(jnp.bfloat16)
    to_owners(lambda head: [(kn.at[:, lanes(head * 128)], kx.at[own_rows, pl.ds(0, 128)], s_k, k_sem)])
    q_rate = lax.rsqrt(both[:, 0:1] / HD + 1e-06)
    qn[...] = (qf[...].astype(jnp.float32) * q_rate * q_gain[...].reshape(1, WIDE)).astype(jnp.bfloat16)

    def send_q(chunk, carry):
        to_owners(
            lambda head: [
                (
                    qn.at[rows(chunk * PART, PART), lanes(head * 128)],
                    qx.at[chunk, rows(place * PART, PART), pl.ds(0, 128)],
                    s_q,
                    q_sem.at[chunk],
                )
            ]
        )
        return carry

    lax.fori_loop(0, CHUNKS, send_q, 0)

    @pl.when(owner)
    def _():
        lane = lax.broadcasted_iota(jnp.int32, (1, 128), 1)
        first = jnp.zeros((1, 128), jnp.int32)
        last = jnp.zeros((1, 128), jnp.int32)
        end = jnp.int32(0)
        for clip in range(CLIPS):
            first = jnp.where(lane == clip, end, first)
            end = end + lens[0, clip]
            last = jnp.where(lane == clip, end, last)
        one = jnp.ones((), jnp.float32)
        zero = jnp.zeros((), jnp.float32)
        frame = lax.broadcasted_iota(jnp.int32, (TOKENS, 128), 0) // TOK_FRAME
        kx[:, 128:256] = jnp.where((frame >= first) & (frame < last), one, zero).astype(jnp.bfloat16)
        vx[:, 128:256] = jnp.ones((TOKENS, 128), jnp.bfloat16)
        for chunk in range(CHUNKS):
            frame = lax.broadcasted_iota(jnp.int32, (BLOCK, 128), 0) // PART * (ROWS // TOK_FRAME) + chunk * PART // TOK_FRAME
            off = jnp.logical_not((frame >= first) & (frame < last)) & (lane < CLIPS)
            qx[chunk, :, 128:256] = jnp.where(off, MASKED * one, zero).astype(jnp.bfloat16)
        pltpu.make_async_copy(vx.at[:, pl.ds(0, 128)], vx.at[:, pl.ds(0, 128)], v_sem).wait()
        pltpu.make_async_copy(kx.at[:, pl.ds(0, 128)], kx.at[:, pl.ds(0, 128)], k_sem).wait()

    loads[2].wait()
    give_w.wait()
    factor = HEAD_DIM ** (-0.5) * 1.4426950408889634

    def step(t, carry):
        @pl.when(owner & (t < CHUNKS))
        def _():
            chunk = t
            pltpu.make_async_copy(
                qx.at[chunk, :, pl.ds(0, 128)], qx.at[chunk, :, pl.ds(0, 128)], q_sem.at[chunk]
            ).wait()

            queries = qx[chunk]
            best, summed = None, None
            for first in range(0, TOKENS, KEYS):
                span = pl.ds(first, KEYS)
                score = lax.dot_general(
                    queries, kx[span, :], (((1,), (1,)), ((), ())), preferred_element_type=jnp.float32
                )
                top = jnp.max(score, axis=1, keepdims=True)
                if first:
                    top = jnp.maximum(best, top)
                weights = jnp.exp2((score - top) * factor).astype(jnp.bfloat16)
                added = jnp.dot(weights, vx[span, :], preferred_element_type=jnp.float32)
                summed = summed * jnp.exp2((best - top) * factor) + added if first else added
                best = top
            back[chunk] = (summed[:, :128] / summed[:, 128:]).astype(jnp.bfloat16)

            to_core = chunk % 2

            def give(i, carry):
                to = (place + i) % SEQ
                src = back.at[chunk, rows(to * PART, PART)]
                dst = ag.at[chunk // 2, rows(group * PART, PART), lanes((core * HERE + mine) * 128)]
                here = (i == 0) & (to_core == core)

                @pl.when(here)
                def _():
                    pltpu.make_async_copy(src, dst, r_sem.at[chunk // 2]).start()

                @pl.when(jnp.logical_not(here))
                def _():
                    pltpu.make_async_remote_copy(
                        src, dst, s_r, r_sem.at[chunk // 2], device_id=(to, to_core, group), device_id_type=MESH
                    ).start()

                return carry

            lax.fori_loop(0, SEQ, give, 0)

        def slot_of(lag):
            chunk = t - lag
            return chunk // 2, (chunk >= 0) & (chunk < CHUNKS) & (chunk % 2 == core)

        slot_home, now_home = slot_of(LAG_HOME)

        @pl.when(now_home)
        def _():
            block = ag.at[slot_home, rows(group * PART, PART)]
            pltpu.make_async_copy(block, block, r_sem.at[slot_home]).wait()
            for to, sem in ((right, left_sem), (left, right_sem)):
                pltpu.make_async_remote_copy(
                    block, block, s_x, sem.at[slot_home], device_id=(place, core, to), device_id_type=MESH
                ).start()
            rest = att_out.at[0, rows((2 * slot_home + core) * PART, PART)]
            pltpu.make_async_remote_copy(
                block.at[:, lanes(other * WIDE, WIDE)], rest, s_a, a_sem,
                device_id=(place, other, group), device_id_type=MESH,
            ).start()
            pltpu.make_async_copy(block.at[:, lanes(core * WIDE, WIDE)], rest, a_sem).start()

        slot_out, now_out = slot_of(LAG_OUT)

        @pl.when(now_out)
        def _():
            block = ag.at[slot_out, rows((group + 2) % 4 * PART, PART)]
            pltpu.make_async_copy(block, block, far_sem.at[slot_out]).wait()
            total = jnp.dot(ag[slot_out], w2[...], preferred_element_type=jnp.float32)
            res[rows(slot_out * 4 * PART, 4 * PART), :] = total.astype(jnp.bfloat16)
            to_core = group // 2
            dst = proj_out.at[0, rows((2 * slot_out + core) * PART, PART), lanes((group % 2) * WIDE, WIDE)]
            for i in (2, 1, 3, 0):
                to = (group + i) % 4
                src = res.at[rows((slot_out * 4 + to) * PART, PART)]

                def far(src=src, to=to):
                    pltpu.make_async_remote_copy(
                        src, dst, s_o, o_sem, device_id=(place, to_core, to), device_id_type=MESH
                    ).start()

                if i:
                    far()
                else:
                    pl.when(to_core != core)(far)

                    @pl.when(to_core == core)
                    def _(src=src):
                        pltpu.make_async_copy(src, dst, o_sem).start()

        slot_line, now_line = slot_of(LAG_LINE)

        @pl.when(now_line)
        def _():
            for source, to, sem, first in ((left, right, left_sem, 0), (right, left, right_sem, WIDE)):
                block = ag.at[slot_line, rows(source * PART, PART)]
                pltpu.make_async_copy(block, block, sem.at[slot_line]).wait()
                half = block.at[:, pl.ds(first, WIDE)]
                pltpu.make_async_remote_copy(
                    half, half, s_f, far_sem.at[slot_line], device_id=(place, core, to), device_id_type=MESH
                ).start()

        return carry

    lax.fori_loop(0, CHUNKS + LAG_OUT, step, 0)

    def done(ref, sem):
        pltpu.make_async_copy(ref, ref, sem).wait()

    @pl.when(owner)
    def _():
        for sem in (s_v, s_k, s_q):
            done(kn.at[:, pl.ds(0, 9 * 128)], sem)
        done(kx.at[pl.ds(0, TOKENS - ROWS // 2), pl.ds(0, 128)], s_r)

    @pl.when(jnp.logical_not(owner))
    def _():
        for sem in (s_v, s_k, s_q):
            done(kn, sem)

    done(ag.at[:, pl.ds(0, 2 * PART)], s_x)
    done(ag.at[:, pl.ds(0, PART)], s_f)
    done(ag.at[:, pl.ds(0, PART), pl.ds(0, WIDE)], s_a)

    @pl.when(group // 2 == core)
    def _():
        done(res.at[pl.ds(0, 3 * SLOTS * PART)], s_o)

    @pl.when(group // 2 != core)
    def _():
        done(res, s_o)

    done(att_out, a_sem)
    done(proj_out, o_sem)


def body(queries, keys, values, q_gain, k_gain, clip_frames, out_weight):
    anywhere = pl.BlockSpec(memory_space=pl.ANY)
    vmem = pl.BlockSpec(memory_space=pltpu.VMEM)
    bf16, f32 = jnp.bfloat16, jnp.float32
    dma = pltpu.SemaphoreType.DMA
    attended, projected = pl.pallas_call(
        kernel,
        out_shape=(pltpu.VMEM((1, ROWS, WIDE), bf16), pltpu.VMEM((1, ROWS, 2 * WIDE), bf16)),
        in_specs=[pl.BlockSpec(memory_space=pltpu.SMEM), anywhere, anywhere, anywhere, vmem, vmem, anywhere],
        out_specs=(vmem, vmem),
        scratch_shapes=[
            pltpu.VMEM((ROWS, WIDE), bf16),
            pltpu.VMEM((ROWS, WIDE), bf16),
            pltpu.VMEM((ROWS, WIDE), bf16),
            pltpu.VMEM((ROWS, WIDE), bf16),
            pltpu.VMEM((2, ROWS, 128), f32),
            pltpu.VMEM((CHUNKS, BLOCK, 256), bf16),
            pltpu.VMEM((TOKENS, 256), bf16),
            pltpu.VMEM((TOKENS, 256), bf16),
            pltpu.VMEM((CHUNKS, BLOCK, 128), bf16),
            pltpu.VMEM((SLOTS, 4 * PART, HD), bf16),
            pltpu.VMEM((HD, WIDE), bf16),
            pltpu.VMEM((SLOTS * 4 * PART, WIDE), bf16),
            dma((3,)), dma, dma, dma, dma, dma((CHUNKS,)), dma((SLOTS,)), dma((SLOTS,)), dma((SLOTS,)), dma((SLOTS,)), dma, dma,
            dma, dma, dma, dma, dma, dma, dma, dma, dma, dma,
        ],
        compiler_params=pltpu.CompilerParams(
            collective_id=0, has_side_effects=True, vmem_limit_bytes=56 << 20
        ),
        cost_estimate=pl.CostEstimate(flops=3 * 10**9, bytes_accessed=8 << 20, transcendentals=4 << 20),
    )(clip_frames, queries, keys, values, q_gain, k_gain, out_weight)
    return attended, projected


def solution(mesh):
    in_specs = (
        P("clip", "seq", "head"),
        P("clip", "seq", "head"),
        P("clip", "seq", "head"),
        P("head"),
        P("head"),
        P("clip", None),
        P("head", "clip"),
    )
    out_specs = (P("clip", "seq", "head"), P("clip", "seq", "head"))
    return jax.shard_map(body, mesh=mesh, in_specs=in_specs, out_specs=out_specs, check_vma=False)
```

time: 69.2 us -> 60 us (0.87)
  local copies, waits for them, and re-layouts: 6.27 us -> 1.56 us
  Pallas kernels: 61.9 us -> 57.6 us
    pallas_call x1, Pallas kernels: 61.9 us -> 57.6 us  [body(): pl.pallas_call(kernel, out_shape=(pltpu.VMEM((1, ROWS, WIDE), bf16), pltp...]
    broadcast_in_dim x2 -> x0, local copies, waits for them, and re-layouts: 2.59 us -> none  [the longest x1 1.29 us: body(): q_gain[None]]
    unnamed x2, local copies, waits for them, and re-layouts: 3.68 us -> 1.56 us
where the time goes in v2:
time: 60 us; the launch traced here: 59.8 us
  Pallas kernels  57.6 us (96%)
  local copies, waits for them, and re-layouts  1.56 us (3%)
  between operations  0.64 us (1%)
    pallas_call x1, Pallas kernels, body(): pl.pallas_call(kernel, out_shape=(pltpu.VMEM((1, ROWS, WIDE), bf16), pltp...  57.6 us
    unnamed x2, local copies, waits for them, and re-layouts  1.56 us

profile of v2, /device:TPU:1, one launch (start us, length us, event | category | flops | bytes accessed | tf_op | source)
XLA Modules:
  0.0 59.8 jit_solution(16843931431966880643)
XLA Ops:
  0.6 57.6 %shard_map.86 = (bf16[1,128,1280]{2,1,0:T(8,128)(2,1)S(1)}, bf16[1,128,2560]{2,1,0:T(8,128)(2,1)S(1)}) custom-call(s32[1,8]{1,0:T(1,128)} %lens.1, bf16[1,128,1280]{2,1,0:T(8,128)(2,1)} %q_in.1, bf16[1,128,1280]{2,1,0:T(8,128)(2,1)} %k_in.1, bf16[1,128,1280]{2,1,0:T(8,128)(2,1)} %v_in.1, f32[1280]{0:T(1024)} %q_gain.1, f32[1280]{0:T(1024)} %k_gain.1, ...), custom_call_target="tpu_custom_call" | custom-call | flops 3000000000 | bytes 8388608 | tf_op jit(solution)/shard_map/pallas_call | solution.py:323
  58.3 0.7 %copy.11 = bf16[1,128,1280]{2,1,0:T(8,128)(2,1)} copy(bf16[1,128,1280]{2,1,0:T(8,128)(2,1)S(1)} %get-tuple-element.2) | data formatting | bytes 655360
  59.0 0.8 %copy.12 = bf16[1,128,2560]{2,1,0:T(8,128)(2,1)} copy(bf16[1,128,2560]{2,1,0:T(8,128)(2,1)S(1)} %get-tuple-element.3) | data formatting | bytes 1310720

commit v3 on v2

--- a/solution.py
+++ b/solution.py
@@ -20,7 +20,10 @@
 BLOCK = SEQ * PART
 KEYS = 512
 TOKENS = SEQ * ROWS
-LAG_HOME, LAG_LINE, LAG_OUT = 3, 6, 11
+QUART = 384
+NARROW = 256
+LAG_HOME, LAG_OUT = 3, 8
+STEP_FAR = 5
 MASKED = -1e30
 MESH = pl.DeviceIdType.MESH
 
@@ -52,14 +55,23 @@
 
 def kernel(
     lens, q_in, k_in, v_in, q_gain, k_gain, w_in, att_out, proj_out,
-    qf, kf, qn, kn, sums, qx, kx, vx, back, ag, w2, res,
-    load_sem, sum_sem, w_sem, v_sem, k_sem, q_sem, r_sem, left_sem, right_sem, far_sem, o_sem, a_sem,
-    s_sum, s_w, s_v, s_k, s_q, s_r, s_x, s_f, s_o, s_a,
+    qf, kf, qn, kn, sums, qx, kx, vx, back, ag, w2, w4, res, res4,
+    load_sem, sum_sem, w_sem, v_sem, k_sem, q_sem, r_sem, near_sem, row_sem, o_sem, a_sem, f_sem, g_sem,
+    s_sum, s_w, s_v, s_k, s_q, s_r, s_x, s_y, s_o, s_p, s_a, s_f, s_g,
 ):
     place, core, group = lax.axis_index("seq"), lax.axis_index("head"), lax.axis_index("clip")
     other = 1 - core
     mine = owned_by(core, place)
     owner = mine >= 0
+    z, y = place // 4, place % 4
+    left, right, far = (group + 3) % 4, (group + 1) % 4, (group + 2) % 4
+    part = (y + z) % 4
+
+    def row_peer(step):
+        along_y = z * 4 + (y + step) % 4
+        along_z = (z + step) % 4 * 4 + y
+        return jnp.where(core == 0, along_y, along_z)
+
 
     loads = [
         pltpu.make_async_copy(q_in.at[0], qf, load_sem.at[0]),
@@ -79,8 +91,7 @@
     lax.fori_loop(1, SEQ, greet_plane, 0)
     pl.semaphore_signal(barrier, inc=1, device_id=(place, other, group), device_id_type=MESH)
 
-    left, right = (group + 3) % 4, (group + 1) % 4
-    for to in (left, right):
+    for to in (left, right, far):
         pl.semaphore_signal(barrier, inc=1, device_id=(place, core, to), device_id_type=MESH)
     loads[0].wait()
     loads[1].wait()
@@ -90,7 +101,7 @@
     sum_k = jnp.sum(k_float * k_float, axis=1, keepdims=True)
     low = lax.broadcasted_iota(jnp.int32, (ROWS, 128), 1) < 64
     sums[0] = jnp.where(low, sum_q, sum_k)
-    pl.semaphore_wait(barrier, SEQ - 1 + 1 + 2)
+    pl.semaphore_wait(barrier, SEQ - 1 + 1 + 3)
 
     def to_owners(copies):
         def one(i, carry):
@@ -125,6 +136,15 @@
         device_id=(place, other, group), device_id_type=MESH,
     )
     give_w.start()
+    my_rows = w4.at[rows(core * WIDE, WIDE)]
+    give_far = pltpu.make_async_remote_copy(
+        w_in.at[:, lanes(jnp.minimum(part * QUART, WIDE - QUART), QUART)], my_rows, s_f, f_sem,
+        device_id=(place, core, far), device_id_type=MESH,
+    )
+    give_far.start()
+    pass_far = pltpu.make_async_remote_copy(
+        my_rows, my_rows, s_g, g_sem, device_id=(place, other, group), device_id_type=MESH
+    )
     give_sums.wait()
     both = sums[0] + sums[1]
     k_rate = lax.rsqrt(both[:, 64:65] / HD + 1e-06)
@@ -203,7 +223,7 @@
             def give(i, carry):
                 to = (place + i) % SEQ
                 src = back.at[chunk, rows(to * PART, PART)]
-                dst = ag.at[chunk // 2, rows(group * PART, PART), lanes((core * HERE + mine) * 128)]
+                dst = ag.at[chunk // 2, pl.ds(2 * PART, PART), lanes((core * HERE + mine) * 128)]
                 here = (i == 0) & (to_core == core)
 
                 @pl.when(here)
@@ -228,11 +248,17 @@
 
         @pl.when(now_home)
         def _():
-            block = ag.at[slot_home, rows(group * PART, PART)]
+            block = ag.at[slot_home, pl.ds(2 * PART, PART)]
             pltpu.make_async_copy(block, block, r_sem.at[slot_home]).wait()
-            for to, sem in ((right, left_sem), (left, right_sem)):
+            for i, to in enumerate((right, left)):
                 pltpu.make_async_remote_copy(
-                    block, block, s_x, sem.at[slot_home], device_id=(place, core, to), device_id_type=MESH
+                    block, ag.at[slot_home, pl.ds(i * PART, PART)], s_x, near_sem.at[slot_home],
+                    device_id=(place, core, to), device_id_type=MESH,
+                ).start()
+            for i in range(1, 4):
+                pltpu.make_async_remote_copy(
+                    block, ag.at[slot_home, pl.ds((2 + i) * PART, PART)], s_y, row_sem.at[slot_home],
+                    device_id=(row_peer(i), core, group), device_id_type=MESH,
                 ).start()
             rest = att_out.at[0, rows((2 * slot_home + core) * PART, PART)]
             pltpu.make_async_remote_copy(
@@ -241,45 +267,76 @@
             ).start()
             pltpu.make_async_copy(block.at[:, lanes(core * WIDE, WIDE)], rest, a_sem).start()
 
+        @pl.when(t == STEP_FAR)
+        def _():
+            give_far.wait()
+            pass_far.start()
+
+        @pl.when(t == LAG_OUT)
+        def _():
+            pass_far.wait()
+
         slot_out, now_out = slot_of(LAG_OUT)
 
         @pl.when(now_out)
         def _():
-            block = ag.at[slot_out, rows((group + 2) % 4 * PART, PART)]
-            pltpu.make_async_copy(block, block, far_sem.at[slot_out]).wait()
-            total = jnp.dot(ag[slot_out], w2[...], preferred_element_type=jnp.float32)
-            res[rows(slot_out * 4 * PART, 4 * PART), :] = total.astype(jnp.bfloat16)
+            token_rows = rows((2 * slot_out + core) * PART, PART)
+
+            two = ag.at[slot_out, pl.ds(0, 2 * PART)]
+            pltpu.make_async_copy(two, two, near_sem.at[slot_out]).wait()
+            total = jnp.dot(ag[slot_out, 0 : 3 * PART, :], w2[...], preferred_element_type=jnp.float32)
+            res[slot_out] = total.astype(jnp.bfloat16)
             to_core = group // 2
-            dst = proj_out.at[0, rows((2 * slot_out + core) * PART, PART), lanes((group % 2) * WIDE, WIDE)]
-            for i in (2, 1, 3, 0):
-                to = (group + i) % 4
-                src = res.at[rows((slot_out * 4 + to) * PART, PART)]
-
-                def far(src=src, to=to):
+            dst = proj_out.at[0, token_rows, lanes((group % 2) * WIDE, WIDE)]
+            for i, to in enumerate((left, right)):
+                pltpu.make_async_remote_copy(
+                    res.at[slot_out, pl.ds(i * PART, PART)], dst, s_o, o_sem,
+                    device_id=(place, to_core, to), device_id_type=MESH,
+                ).start()
+            src = res.at[slot_out, pl.ds(2 * PART, PART)]
+
+            @pl.when(to_core == core)
+            def _():
+                pltpu.make_async_copy(src, dst, o_sem).start()
+
+            @pl.when(to_core != core)
+            def _():
+                pltpu.make_async_remote_copy(
+                    src, dst, s_o, o_sem, device_id=(place, to_core, group), device_id_type=MESH
+                ).start()
+
+            three = ag.at[slot_out, pl.ds(3 * PART, 3 * PART)]
+            pltpu.make_async_copy(three, three, row_sem.at[slot_out]).wait()
+            total = jnp.dot(ag[slot_out, 2 * PART :, :], w4[...], preferred_element_type=jnp.float32)
+            res4[slot_out] = total.astype(jnp.bfloat16)
+            far_core = far // 2
+
+            def give_part(width, first, column):
+                far_dst = proj_out.at[0, token_rows, lanes((far % 2) * WIDE + column, width)]
+                for i in range(1, 4):
                     pltpu.make_async_remote_copy(
-                        src, dst, s_o, o_sem, device_id=(place, to_core, to), device_id_type=MESH
+                        res4.at[slot_out, pl.ds(i * PART, PART), lanes(first, width)], far_dst, s_p, o_sem,
+                        device_id=(row_peer(4 - i), far_core, group), device_id_type=MESH,
                     ).start()
-
-                if i:
-                    far()
-                else:
-                    pl.when(to_core != core)(far)
-
-                    @pl.when(to_core == core)
-                    def _(src=src):
-                        pltpu.make_async_copy(src, dst, o_sem).start()
-
-        slot_line, now_line = slot_of(LAG_LINE)
-
-        @pl.when(now_line)
-        def _():
-            for source, to, sem, first in ((left, right, left_sem, 0), (right, left, right_sem, WIDE)):
-                block = ag.at[slot_line, rows(source * PART, PART)]
-                pltpu.make_async_copy(block, block, sem.at[slot_line]).wait()
-                half = block.at[:, pl.ds(first, WIDE)]
-                pltpu.make_async_remote_copy(
-                    half, half, s_f, far_sem.at[slot_line], device_id=(place, core, to), device_id_type=MESH
-                ).start()
+                far_src = res4.at[slot_out, pl.ds(0, PART), lanes(first, width)]
+
+                @pl.when(far_core == core)
+                def _():
+                    pltpu.make_async_copy(far_src, far_dst, o_sem).start()
+
+                @pl.when(far_core != core)
+                def _():
+                    pltpu.make_async_remote_copy(
+                        far_src, far_dst, s_p, o_sem, device_id=(place, far_core, group), device_id_type=MESH
+                    ).start()
+
+            @pl.when(part < 2)
+            def _():
+                give_part(QUART, 0, part * QUART)
+
+            @pl.when(part >= 2)
+            def _():
+                give_part(NARROW, (part - 2) * 128, 2 * QUART + (part - 2) * NARROW)
 
         return carry
 
@@ -300,16 +357,22 @@
             done(kn, sem)
 
     done(ag.at[:, pl.ds(0, 2 * PART)], s_x)
-    done(ag.at[:, pl.ds(0, PART)], s_f)
+    done(ag.at[:, pl.ds(0, 3 * PART)], s_y)
     done(ag.at[:, pl.ds(0, PART), pl.ds(0, WIDE)], s_a)
 
-    @pl.when(group // 2 == core)
-    def _():
-        done(res.at[pl.ds(0, 3 * SLOTS * PART)], s_o)
-
-    @pl.when(group // 2 != core)
-    def _():
-        done(res, s_o)
+    for is_here, near_rows, far_rows in ((True, 2 * PART, 4 * PART), (False, 3 * PART, 3 * PART)):
+
+        @pl.when((group // 2 == core) == is_here)
+        def _(near_rows=near_rows, far_rows=far_rows):
+            done(res.at[:, pl.ds(0, near_rows)], s_o)
+
+            @pl.when(part < 2)
+            def _():
+                done(res4.at[:, pl.ds(0, far_rows)], s_p)
+
+            @pl.when(part >= 2)
+            def _():
+                done(res4.at[:, pl.ds(0, far_rows), pl.ds(0, NARROW)], s_p)
 
     done(att_out, a_sem)
     done(proj_out, o_sem)
@@ -335,11 +398,13 @@
             pltpu.VMEM((TOKENS, 256), bf16),
             pltpu.VMEM((TOKENS, 256), bf16),
             pltpu.VMEM((CHUNKS, BLOCK, 128), bf16),
-            pltpu.VMEM((SLOTS, 4 * PART, HD), bf16),
+            pltpu.VMEM((SLOTS, 6 * PART, HD), bf16),
             pltpu.VMEM((HD, WIDE), bf16),
-            pltpu.VMEM((SLOTS * 4 * PART, WIDE), bf16),
-            dma((3,)), dma, dma, dma, dma, dma((CHUNKS,)), dma((SLOTS,)), dma((SLOTS,)), dma((SLOTS,)), dma((SLOTS,)), dma, dma,
-            dma, dma, dma, dma, dma, dma, dma, dma, dma, dma,
+            pltpu.VMEM((HD, QUART), bf16),
+            pltpu.VMEM((SLOTS, 3 * PART, WIDE), bf16),
+            pltpu.VMEM((SLOTS, 4 * PART, QUART), bf16),
+            dma((3,)), dma, dma, dma, dma, dma((CHUNKS,)), dma((SLOTS,)), dma((SLOTS,)), dma((SLOTS,)), dma, dma, dma, dma,
+            dma, dma, dma, dma, dma, dma, dma, dma, dma, dma, dma, dma, dma,
         ],
         compiler_params=pltpu.CompilerParams(
             collective_id=0, has_side_effects=True, vmem_limit_bytes=56 << 20

time: 60 us -> 56.5 us (0.942)
  Pallas kernels: 57.6 us -> 54.2 us
    pallas_call x1, Pallas kernels: 57.6 us -> 54.2 us  [body(): pl.pallas_call(kernel, out_shape=(pltpu.VMEM((1, ROWS, WIDE), bf16), pltp...]
where the time goes in v3:
time: 56.5 us; the launch traced here: 56.4 us
  Pallas kernels  54.2 us (96%)
  local copies, waits for them, and re-layouts  1.56 us (3%)
  between operations  0.64 us (1%)
    pallas_call x1, Pallas kernels, body(): pl.pallas_call(kernel, out_shape=(pltpu.VMEM((1, ROWS, WIDE), bf16), pltp...  54.2 us
    unnamed x2, local copies, waits for them, and re-layouts  1.56 us

profile of v3, /device:TPU:1, one launch (start us, length us, event | category | flops | bytes accessed | tf_op | source)
XLA Modules:
  0.0 56.4 jit_solution(12124437637017809103)
XLA Ops:
  0.6 54.2 %shard_map.86 = (bf16[1,128,1280]{2,1,0:T(8,128)(2,1)S(1)}, bf16[1,128,2560]{2,1,0:T(8,128)(2,1)S(1)}) custom-call(s32[1,8]{1,0:T(1,128)} %lens.1, bf16[1,128,1280]{2,1,0:T(8,128)(2,1)} %q_in.1, bf16[1,128,1280]{2,1,0:T(8,128)(2,1)} %k_in.1, bf16[1,128,1280]{2,1,0:T(8,128)(2,1)} %v_in.1, f32[1280]{0:T(1024)} %q_gain.1, f32[1280]{0:T(1024)} %k_gain.1, ...), custom_call_target="tpu_custom_call" | custom-call | flops 3000000000 | bytes 8388608 | tf_op jit(solution)/shard_map/pallas_call | solution.py:386
  54.8 0.7 %copy.11 = bf16[1,128,1280]{2,1,0:T(8,128)(2,1)} copy(bf16[1,128,1280]{2,1,0:T(8,128)(2,1)S(1)} %get-tuple-element.2) | data formatting | bytes 655360
  55.6 0.8 %copy.12 = bf16[1,128,2560]{2,1,0:T(8,128)(2,1)} copy(bf16[1,128,2560]{2,1,0:T(8,128)(2,1)S(1)} %get-tuple-element.3) | data formatting | bytes 1310720

commit v4 on v3

--- a/solution.py
+++ b/solution.py
@@ -22,8 +22,8 @@
 TOKENS = SEQ * ROWS
 QUART = 384
 NARROW = 256
-LAG_HOME, LAG_OUT = 3, 8
-STEP_FAR = 5
+LAG_HOME, LAG_OUT = 3, 7
+STEP_FAR = 4
 MASKED = -1e30
 MESH = pl.DeviceIdType.MESH
 
@@ -105,7 +105,7 @@
 
     def to_owners(copies):
         def one(i, carry):
-            head = (i + place) % HERE
+            head = (3 * i + place) % HERE
             to = owner_of(core, head)
 
             @pl.when(to == place)
@@ -190,8 +190,6 @@
         pltpu.make_async_copy(vx.at[:, pl.ds(0, 128)], vx.at[:, pl.ds(0, 128)], v_sem).wait()
         pltpu.make_async_copy(kx.at[:, pl.ds(0, 128)], kx.at[:, pl.ds(0, 128)], k_sem).wait()
 
-    loads[2].wait()
-    give_w.wait()
     factor = HEAD_DIM ** (-0.5) * 1.4426950408889634
 
     def step(t, carry):
@@ -274,6 +272,8 @@
 
         @pl.when(t == LAG_OUT)
         def _():
+            loads[2].wait()
+            give_w.wait()
             pass_far.wait()
 
         slot_out, now_out = slot_of(LAG_OUT)

time: 56.5 us -> 56.8 us (level)
  no operation moved by 1% of the time
where the time goes in v4:
time: 56.8 us; the launch traced here: 56.6 us
  Pallas kernels  54.4 us (96%)
  local copies, waits for them, and re-layouts  1.56 us (3%)
  between operations  0.64 us (1%)
    pallas_call x1, Pallas kernels, body(): pl.pallas_call(kernel, out_shape=(pltpu.VMEM((1, ROWS, WIDE), bf16), pltp...  54.4 us
    unnamed x2, local copies, waits for them, and re-layouts  1.56 us

profile of v4, /device:TPU:1, one launch (start us, length us, event | category | flops | bytes accessed | tf_op | source)
XLA Modules:
  0.0 56.6 jit_solution(6132625060219237088)
XLA Ops:
  0.6 54.4 %shard_map.86 = (bf16[1,128,1280]{2,1,0:T(8,128)(2,1)S(1)}, bf16[1,128,2560]{2,1,0:T(8,128)(2,1)S(1)}) custom-call(s32[1,8]{1,0:T(1,128)} %lens.1, bf16[1,128,1280]{2,1,0:T(8,128)(2,1)} %q_in.1, bf16[1,128,1280]{2,1,0:T(8,128)(2,1)} %k_in.1, bf16[1,128,1280]{2,1,0:T(8,128)(2,1)} %v_in.1, f32[1280]{0:T(1024)} %q_gain.1, f32[1280]{0:T(1024)} %k_gain.1, ...), custom_call_target="tpu_custom_call" | custom-call | flops 3000000000 | bytes 8388608 | tf_op jit(solution)/shard_map/pallas_call | solution.py:386
  55.1 0.7 %copy.11 = bf16[1,128,1280]{2,1,0:T(8,128)(2,1)} copy(bf16[1,128,1280]{2,1,0:T(8,128)(2,1)S(1)} %get-tuple-element.2) | data formatting | bytes 655360
  55.8 0.8 %copy.12 = bf16[1,128,2560]{2,1,0:T(8,128)(2,1)} copy(bf16[1,128,2560]{2,1,0:T(8,128)(2,1)S(1)} %get-tuple-element.3) | data formatting | bytes 1310720
